TPU v7x, 256 devices: a whole 4x4x8 slice. The times are simulated.
256 devices in a mesh: row: 8 (over x, core), axial: 32 (over z, y).
Axes of the slice: x: 4, y: 4, z: 8, core: 2. Of those that a mesh axis runs over, the one named last changes fastest.
Arguments:
- prior_warmth: float32 [1024, 128, 256], P('axial', 'row'), may hold values from -6 to 6
- tube_supply: float32 [1024, 128, 256], P('axial', 'row'), may hold values from -6 to 7
- lower_coupling: float32 [1024, 128, 256], P('axial', 'row'), may hold values from 4096 to 32768
- higher_coupling: float32 [1024, 128, 256], P('axial', 'row'), may hold values from 4096 to 32768
- void_ratio: float32 [4], replicated, may hold values from 0.1 to 1
- void_group: int32 [128, 256], P('row'), may hold values from 0 to 3
- baffle_region: int32 [1024], P('axial'), may hold values from 0 to 31, never falling along the last dimension, each value on 1 to 64 neighbouring positions
- transverse_sense: int32 [32], replicated, may hold values from 0 to 1
Outputs:
- temperature_new: float32 [1024, 128, 256], P('axial', 'row')
Inputs may be any that keep to these rules, and one draw needn't show every extreme that they name: `baffle_region`: zone ids never fall along the axial dimension; every zone holds at least one slab.
All inputs are finite; a program needn't handle non-finite values.
Results may differ from a plain program's by a relative error of at most 0.0011.
Values sent between devices are 32-bit elements; how exact they have to be, the bound alone decides.
A program may use at most 64 MiB of HBM per device.

v0:
```python
import jax
import jax.numpy as jnp
from jax import lax
from jax.sharding import PartitionSpec as P

transverse_speed = 0.35
mixing_coefficient = 0.15
supplied_power = 0.5
axial_drift = 64.0


def extended(block, sides, width):
    for axis, dim in sides:
        count = lax.axis_size(axis)
        forward = [(i, i + 1) for i in range(count - 1)]
        backward = [(target, source) for source, target in forward]
        low = lax.ppermute(
            lax.slice_in_dim(block, block.shape[dim] - width, None, axis=dim), axis, forward
        )
        high = lax.ppermute(lax.slice_in_dim(block, 0, width, axis=dim), axis, backward)
        block = jnp.concatenate([low, block, high], axis=dim)
    return block


def from_behind(array, axis, by):
    length = lax.axis_size(axis)
    pairs = [(i, i + by) for i in range(length) if 0 <= i + by < length]
    return lax.ppermute(array, axis, pairs)


def from_earlier(values, stride):
    return jnp.concatenate([jnp.zeros_like(values[:stride]), values[:-stride]], 0)


def from_later(values, stride):
    return jnp.concatenate([values[stride:], jnp.zeros_like(values[:stride])], 0)


def reduce_rows(low_band, main_band, high_band, right_hand):
    row_count = low_band.shape[0]
    stride = 1
    while stride < row_count:
        ratio_low = low_band / main_band
        ratio_high = high_band / main_band
        ratio_rhs = right_hand / main_band
        new_low = -low_band * from_earlier(ratio_low, stride)
        new_high = -high_band * from_later(ratio_high, stride)
        main_band = (
            main_band
            - low_band * from_earlier(ratio_high, stride)
            - high_band * from_later(ratio_low, stride)
        )
        right_hand = (
            right_hand
            - low_band * from_earlier(ratio_rhs, stride)
            - high_band * from_later(ratio_rhs, stride)
        )
        low_band, high_band = (new_low, new_high)
        stride = stride * 2
    return right_hand / main_band


def on_device(
    prior_warmth,
    tube_supply,
    lower_coupling,
    higher_coupling,
    void_ratio,
    void_group,
    baffle_region,
    transverse_sense,
):
    slab_depth = prior_warmth.shape[0]
    bordered_grid = extended(prior_warmth, (("row", 1),), 1)
    leftside_boundary = bordered_grid[:, :-2]
    right_boundary = bordered_grid[:, 2:]
    sideways_margin = jnp.pad(prior_warmth, ((0, 0), (0, 0), (1, 1)))
    bottom_boundary = sideways_margin[:, :, :-2]
    upper_boundary = sideways_margin[:, :, 2:]
    void_share = jnp.zeros(void_group.shape, jnp.float32)
    for class_number in range(void_ratio.shape[0]):
        void_share = void_share + jnp.where(
            void_group == class_number, void_ratio[class_number], 0.0
        )
    zone_range = lax.iota(jnp.int32, transverse_sense.shape[0])
    elimination_sweep = jnp.sum(
        jnp.where(baffle_region[:, None] == zone_range[None, :], transverse_sense[None, :], 0), 1
    ).astype(jnp.float32)[:, None, None]
    lagged_contribution = (
        prior_warmth
        + transverse_speed
        * void_share
        * (
            elimination_sweep * (leftside_boundary - prior_warmth)
            + (1.0 - elimination_sweep) * (right_boundary - prior_warmth)
        )
        + mixing_coefficient
        * (
            leftside_boundary
            + right_boundary
            + bottom_boundary
            + upper_boundary
            - 4.0 * prior_warmth
        )
        + supplied_power * tube_supply
    )
    low_all = -(lower_coupling + axial_drift)
    high_all = -higher_coupling
    main_all = 1.0 + lower_coupling + higher_coupling + axial_drift
    row_index = lax.iota(jnp.int32, slab_depth)[:, None, None, None]
    is_last = row_index == slab_depth - 1
    is_inner_top = row_index == slab_depth - 2
    is_first = row_index == 0
    low_band = jnp.where(is_last, 0.0, low_all[:, None])
    main_band = jnp.where(is_last, 1.0, main_all[:, None])
    high_band = jnp.where(is_last | is_inner_top, 0.0, high_all[:, None])
    right_hand = jnp.concatenate(
        [
            jnp.where(is_last, 0.0, lagged_contribution[:, None]),
            jnp.where(is_first, -low_all[:, None], 0.0),
            jnp.where(is_inner_top, -high_all[:, None], 0.0),
        ],
        1,
    )
    pieces = reduce_rows(low_band, main_band, high_band, right_hand)
    local_part = pieces[:, 0]
    left_part = pieces[:, 1]
    right_part = pieces[:, 2]
    inner_top_row = slab_depth - 2
    next_first = from_behind(jnp.stack([local_part[0], left_part[0], right_part[0]]), "axial", -1)
    edge_low = low_all[slab_depth - 1]
    edge_high = high_all[slab_depth - 1]
    coupled_low = edge_low * left_part[inner_top_row]
    coupled_main = (
        main_all[slab_depth - 1] + edge_low * right_part[inner_top_row] + edge_high * next_first[1]
    )
    coupled_high = edge_high * next_first[2]
    coupled_rhs = (
        lagged_contribution[slab_depth - 1]
        - edge_low * local_part[inner_top_row]
        - edge_high * next_first[0]
    )
    devices = lax.axis_size("axial")
    stride = 1
    while stride < devices:
        outgoing = jnp.stack(
            [coupled_low / coupled_main, coupled_high / coupled_main, coupled_rhs / coupled_main]
        )
        from_below = from_behind(outgoing, "axial", stride)
        from_above = from_behind(outgoing, "axial", -stride)
        new_low = -coupled_low * from_below[0]
        new_high = -coupled_high * from_above[1]
        coupled_main = coupled_main - coupled_low * from_below[1] - coupled_high * from_above[0]
        coupled_rhs = coupled_rhs - coupled_low * from_below[2] - coupled_high * from_above[2]
        coupled_low, coupled_high = (new_low, new_high)
        stride = stride * 2
    own_edge = coupled_rhs / coupled_main
    prior_edge = from_behind(own_edge, "axial", 1)
    updated = local_part + left_part * prior_edge + right_part * own_edge
    return jnp.where(row_index[:, 0] == slab_depth - 1, own_edge, updated)


def solution(mesh):
    placed = (
        P("axial", "row", None),
        P("axial", "row", None),
        P("axial", "row", None),
        P("axial", "row", None),
        P(),
        P("row", None),
        P("axial"),
        P(),
    )
    return jax.shard_map(
        on_device, mesh=mesh, in_specs=placed, out_specs=P("axial", "row", None), check_vma=False
    )
```

profile of v0, /device:TPU:36, one launch (start us, length us, event | category | flops | bytes accessed | tf_op | source)
XLA Modules:
  0.0 101.3 jit_solution(14028736203000790663)
XLA Ops:
  0.0 1.1 %fusion.81 = (f32[32,1,256]{2,1,0:T(1,128)S(1)}, f32[32,1,256]{2,1,0:T(1,128)S(1)}) fusion(f32[32,16,256]{2,1,0:T(8,128)} %param.8), kind=kLoop, calls=%fused_computation.194 | loop fusion | bytes 131072 | tf_op jit(solution)/shard_map/slice | solution.py:18
  1.1 1.9 %collective-permute-start.1 = (f32[32,1,256]{2,1,0:T(1,128)S(1)}, f32[32,1,256]{2,1,0:T(1,128)S(1)}, u32[]{:S(2)}, u32[]{:S(2)}) collective-permute-start(f32[32,1,256]{2,1,0:T(1,128)S(1)} %get-tuple-element.101), channel_id=1, source_target_pairs={{32,0},{64,32},{96,64},{128,96},{160,128},{192,160},{224,192},{33,... | collective-permute-start | bytes 98312 | tf_op jit(solution)/shard_map/ppermute | solution.py:20
  3.0 2.4 %collective-permute-start = (f32[32,1,256]{2,1,0:T(1,128)S(1)}, f32[32,1,256]{2,1,0:T(1,128)S(1)}, u32[]{:S(2)}, u32[]{:S(2)}) collective-permute-start(f32[32,1,256]{2,1,0:T(1,128)S(1)} %get-tuple-element.100), channel_id=1, source_target_pairs={{0,32},{32,64},{64,96},{96,128},{128,160},{160,192},{192,224},{1,3... | collective-permute-start | bytes 98312 | tf_op jit(solution)/shard_map/ppermute | solution.py:17
  5.4 0.9 select_reduce_fusion
  6.3 1.5 %fusion.86 = (f32[1]{0:T(128)}, f32[1]{0:T(128)}, f32[1]{0:T(128)}, f32[1]{0:T(128)}) fusion(f32[4]{0:T(128)} %param.12), kind=kLoop, calls=%fused_computation.199 | loop fusion | bytes 32 | tf_op jit(solution)/shard_map/slice | solution.py:83
  7.8 3.3 %add_multiply_fusion = f32[16,256]{1,0:T(8,128)S(1)} fusion(s32[16,256]{1,0:T(8,128)} %param.13, f32[]{:T(128)} %bitcast.3, f32[]{:T(128)} %bitcast.2, f32[]{:T(128)} %bitcast.1, f32[]{:T(128)} %bitcast), kind=kLoop, calls=%fused_computation.157 | loop fusion | flops 49152 | bytes 32784 | tf_op jit(solution)/shard_map/mul | solution.py:91
  11.1 3.5 %fusion.78 = (f32[32,16,256]{2,1,0:T(8,128)S(1)}, f32[32,1,16,256]{3,2,0,1:T(8,128)S(1)}, f32[32,16,256]{2,1,0:T(8,128)S(1)}, f32[32,16,256]{2,1,0:T(8,128)S(1)}...) fusion(f32[32,16,256]{2,1,0:T(8,128)} %param.11, ...), kind=kLoop, calls=%fused_computation.191 | loop fusion | flops 3932160 | bytes 7422336 | tf_op jit(solution)/shard_map/neg | solution.py:108
  14.7 0.9 copy-done
  19.0 0.8 broadcast_divide_fusion.3
  20.2 0.9 broadcast_divide_fusion.2
  21.5 0.9 broadcast_divide_fusion.1
  23.1 0.8 broadcast_divide_fusion
  25.0 4.5 %collective-permute-start.2 = (f32[3,16,256]{2,1,0:T(8,128)S(1)}, f32[3,16,256]{2,1,0:T(8,128)S(1)}, u32[]{:S(2)}, u32[]{:S(2)}) collective-permute-start(f32[3,16,256]{2,1,0:T(8,128)S(1)} %pad_maximum_fusion.3), channel_id=1, source_target_pairs={{1,0},{2,1},{3,2},{4,3},{5,4},{6,5},{7,6},{8,7},{9,8},{10,9},{11,1... | collective-permute-start | bytes 147464 | tf_op jit(solution)/shard_map/ppermute | solution.py:28
  29.4 2.0 %collective-permute-done.2 = f32[3,16,256]{2,1,0:T(8,128)S(1)} collective-permute-done((f32[3,16,256]{2,1,0:T(8,128)S(1)}, f32[3,16,256]{2,1,0:T(8,128)S(1)}, u32[]{:S(2)}, u32[]{:S(2)}) %collective-permute-start.2) | collective-permute-done | bytes 49184 | tf_op jit(solution)/shard_map/ppermute | solution.py:28
  31.5 3.4 %collective-permute-start.3 = (f32[3,16,256]{2,1,0:T(8,128)S(1)}, f32[3,16,256]{2,1,0:T(8,128)S(1)}, u32[]{:S(2)}, u32[]{:S(2)}) collective-permute-start(f32[3,16,256]{2,1,0:T(8,128)S(1)} %pad_maximum_fusion.4), channel_id=1, source_target_pairs={{0,1},{1,2},{2,3},{3,4},{4,5},{5,6},{6,7},{7,8},{8,9},{9,10},{10,1... | collective-permute-start | bytes 147464 | tf_op jit(solution)/shard_map/ppermute | solution.py:28
  34.9 5.0 %collective-permute-start.4 = (f32[3,16,256]{2,1,0:T(8,128)S(1)}, f32[3,16,256]{2,1,0:T(8,128)S(1)}, u32[]{:S(2)}, u32[]{:S(2)}) collective-permute-start(f32[3,16,256]{2,1,0:T(8,128)S(1)} %pad_maximum_fusion.4), channel_id=1, source_target_pairs={{1,0},{2,1},{3,2},{4,3},{5,4},{6,5},{7,6},{8,7},{9,8},{10,9},{11,1... | collective-permute-start | bytes 147464 | tf_op jit(solution)/shard_map/ppermute | solution.py:28
  40.1 1.6 %collective-permute-done.4 = f32[3,16,256]{2,1,0:T(8,128)S(1)} collective-permute-done((f32[3,16,256]{2,1,0:T(8,128)S(1)}, f32[3,16,256]{2,1,0:T(8,128)S(1)}, u32[]{:S(2)}, u32[]{:S(2)}) %collective-permute-start.4) | collective-permute-done | bytes 49184 | tf_op jit(solution)/shard_map/ppermute | solution.py:28
  41.7 6.2 %collective-permute-start.5 = (f32[3,16,256]{2,1,0:T(8,128)S(1)}, f32[3,16,256]{2,1,0:T(8,128)S(1)}, u32[]{:S(2)}, u32[]{:S(2)}) collective-permute-start(f32[3,16,256]{2,1,0:T(8,128)S(1)} %pad_maximum_fusion.5), channel_id=1, source_target_pairs={{0,2},{1,3},{2,4},{3,5},{4,6},{5,7},{6,8},{7,9},{8,10},{9,11},{10,... | collective-permute-start | bytes 147464 | tf_op jit(solution)/shard_map/ppermute | solution.py:28
  47.9 2.1 %collective-permute-start.6 = (f32[3,16,256]{2,1,0:T(8,128)S(1)}, f32[3,16,256]{2,1,0:T(8,128)S(1)}, u32[]{:S(2)}, u32[]{:S(2)}) collective-permute-start(f32[3,16,256]{2,1,0:T(8,128)S(1)} %pad_maximum_fusion.5), channel_id=1, source_target_pairs={{2,0},{3,1},{4,2},{5,3},{6,4},{7,5},{8,6},{9,7},{10,8},{11,9},{12,... | collective-permute-start | bytes 147464 | tf_op jit(solution)/shard_map/ppermute | solution.py:28
  50.1 5.3 %collective-permute-done.6 = f32[3,16,256]{2,1,0:T(8,128)S(1)} collective-permute-done((f32[3,16,256]{2,1,0:T(8,128)S(1)}, f32[3,16,256]{2,1,0:T(8,128)S(1)}, u32[]{:S(2)}, u32[]{:S(2)}) %collective-permute-start.6) | collective-permute-done | bytes 49184 | tf_op jit(solution)/shard_map/ppermute | solution.py:28
  55.4 3.8 %collective-permute-start.7 = (f32[3,16,256]{2,1,0:T(8,128)S(1)}, f32[3,16,256]{2,1,0:T(8,128)S(1)}, u32[]{:S(2)}, u32[]{:S(2)}) collective-permute-start(f32[3,16,256]{2,1,0:T(8,128)S(1)} %pad_maximum_fusion.6), channel_id=1, source_target_pairs={{0,4},{1,5},{2,6},{3,7},{4,8},{5,9},{6,10},{7,11},{8,12},{9,13},{1... | collective-permute-start | bytes 147464 | tf_op jit(solution)/shard_map/ppermute | solution.py:28
  59.3 2.0 %collective-permute-start.8 = (f32[3,16,256]{2,1,0:T(8,128)S(1)}, f32[3,16,256]{2,1,0:T(8,128)S(1)}, u32[]{:S(2)}, u32[]{:S(2)}) collective-permute-start(f32[3,16,256]{2,1,0:T(8,128)S(1)} %pad_maximum_fusion.6), channel_id=1, source_target_pairs={{4,0},{5,1},{6,2},{7,3},{8,4},{9,5},{10,6},{11,7},{12,8},{13,9},{1... | collective-permute-start | bytes 147464 | tf_op jit(solution)/shard_map/ppermute | solution.py:28
  61.4 4.9 %collective-permute-done.8 = f32[3,16,256]{2,1,0:T(8,128)S(1)} collective-permute-done((f32[3,16,256]{2,1,0:T(8,128)S(1)}, f32[3,16,256]{2,1,0:T(8,128)S(1)}, u32[]{:S(2)}, u32[]{:S(2)}) %collective-permute-start.8) | collective-permute-done | bytes 49184 | tf_op jit(solution)/shard_map/ppermute | solution.py:28
  66.4 6.5 %collective-permute-start.9 = (f32[3,16,256]{2,1,0:T(8,128)S(1)}, f32[3,16,256]{2,1,0:T(8,128)S(1)}, u32[]{:S(2)}, u32[]{:S(2)}) collective-permute-start(f32[3,16,256]{2,1,0:T(8,128)S(1)} %pad_maximum_fusion.7), channel_id=1, source_target_pairs={{0,8},{1,9},{2,10},{3,11},{4,12},{5,13},{6,14},{7,15},{8,16},{9,17... | collective-permute-start | bytes 147464 | tf_op jit(solution)/shard_map/ppermute | solution.py:28
  72.9 1.3 %collective-permute-start.10 = (f32[3,16,256]{2,1,0:T(8,128)S(1)}, f32[3,16,256]{2,1,0:T(8,128)S(1)}, u32[]{:S(2)}, u32[]{:S(2)}) collective-permute-start(f32[3,16,256]{2,1,0:T(8,128)S(1)} %pad_maximum_fusion.7), channel_id=1, source_target_pairs={{8,0},{9,1},{10,2},{11,3},{12,4},{13,5},{14,6},{15,7},{16,8},{17,9... | collective-permute-start | bytes 147464 | tf_op jit(solution)/shard_map/ppermute | solution.py:28
  74.6 5.2 %collective-permute-done.10 = f32[3,16,256]{2,1,0:T(8,128)S(1)} collective-permute-done((f32[3,16,256]{2,1,0:T(8,128)S(1)}, f32[3,16,256]{2,1,0:T(8,128)S(1)}, u32[]{:S(2)}, u32[]{:S(2)}) %collective-permute-start.10) | collective-permute-done | bytes 49184 | tf_op jit(solution)/shard_map/ppermute | solution.py:28
  79.9 2.5 %collective-permute-start.11 = (f32[3,16,256]{2,1,0:T(8,128)S(1)}, f32[3,16,256]{2,1,0:T(8,128)S(1)}, u32[]{:S(2)}, u32[]{:S(2)}) collective-permute-start(f32[3,16,256]{2,1,0:T(8,128)S(1)} %pad_maximum_fusion.8), channel_id=1, source_target_pairs={{0,16},{1,17},{2,18},{3,19},{4,20},{5,21},{6,22},{7,23},{8,24},{9,... | collective-permute-start | bytes 147464 | tf_op jit(solution)/shard_map/ppermute | solution.py:28
  82.4 1.3 %collective-permute-start.12 = (f32[3,16,256]{2,1,0:T(8,128)S(1)}, f32[3,16,256]{2,1,0:T(8,128)S(1)}, u32[]{:S(2)}, u32[]{:S(2)}) collective-permute-start(f32[3,16,256]{2,1,0:T(8,128)S(1)} %pad_maximum_fusion.8), channel_id=1, source_target_pairs={{16,0},{17,1},{18,2},{19,3},{20,4},{21,5},{22,6},{23,7},{24,8},{25... | collective-permute-start | bytes 147464 | tf_op jit(solution)/shard_map/ppermute | solution.py:28
  84.3 8.3 %collective-permute-done.12 = f32[3,16,256]{2,1,0:T(8,128)S(1)} collective-permute-done((f32[3,16,256]{2,1,0:T(8,128)S(1)}, f32[3,16,256]{2,1,0:T(8,128)S(1)}, u32[]{:S(2)}, u32[]{:S(2)}) %collective-permute-start.12) | collective-permute-done | bytes 49184 | tf_op jit(solution)/shard_map/ppermute | solution.py:28
  92.6 3.4 %collective-permute-start.13 = (f32[16,256]{1,0:T(8,128)S(1)}, f32[16,256]{1,0:T(8,128)S(1)}, u32[]{:S(2)}, u32[]{:S(2)}) collective-permute-start(f32[16,256]{1,0:T(8,128)S(1)} %fusion.36), channel_id=1, source_target_pairs={{0,1},{1,2},{2,3},{3,4},{4,5},{5,6},{6,7},{7,8},{8,9},{9,10},{10,1... | collective-permute-start | bytes 49160 | tf_op jit(solution)/shard_map/ppermute | solution.py:28
  96.1 4.3 %collective-permute-done.13 = f32[16,256]{1,0:T(8,128)S(1)} collective-permute-done((f32[16,256]{1,0:T(8,128)S(1)}, f32[16,256]{1,0:T(8,128)S(1)}, u32[]{:S(2)}, u32[]{:S(2)}) %collective-permute-start.13) | collective-permute-done | bytes 16416 | tf_op jit(solution)/shard_map/ppermute | solution.py:28
  100.3 0.9 fusion.9
  (56 shorter events, 7.6 us)
Async XLA Ops:
  1.1 10.0 %collective-permute-start.1 = (f32[32,1,256]{2,1,0:T(1,128)S(1)}, f32[32,1,256]{2,1,0:T(1,128)S(1)}, u32[]{:S(2)}, u32[]{:S(2)}) collective-permute-start(f32[32,1,256]{2,1,0:T(1,128)S(1)} %get-tuple-element.101), channel_id=1, source_target_pairs={{32,0},{64,32},{96,64},{128,96},{160,128},{192,160},{224,192},{33,... | collective-permute-start | bytes 98312 | tf_op jit(solution)/shard_map/ppermute | solution.py:20
  3.0 8.1 %collective-permute-start = (f32[32,1,256]{2,1,0:T(1,128)S(1)}, f32[32,1,256]{2,1,0:T(1,128)S(1)}, u32[]{:S(2)}, u32[]{:S(2)}) collective-permute-start(f32[32,1,256]{2,1,0:T(1,128)S(1)} %get-tuple-element.100), channel_id=1, source_target_pairs={{0,32},{32,64},{64,96},{96,128},{128,160},{160,192},{192,224},{1,3... | collective-permute-start | bytes 98312 | tf_op jit(solution)/shard_map/ppermute | solution.py:17
  14.6 1.0 %copy-start = (f32[32,16,256]{2,1,0:T(8,128)S(1)}, f32[32,16,256]{2,1,0:T(8,128)}, u32[]{:S(2)}) copy-start(f32[32,16,256]{2,1,0:T(8,128)} %param.10) | copy-start | bytes 1572868
  25.0 6.5 %collective-permute-start.2 = (f32[3,16,256]{2,1,0:T(8,128)S(1)}, f32[3,16,256]{2,1,0:T(8,128)S(1)}, u32[]{:S(2)}, u32[]{:S(2)}) collective-permute-start(f32[3,16,256]{2,1,0:T(8,128)S(1)} %pad_maximum_fusion.3), channel_id=1, source_target_pairs={{1,0},{2,1},{3,2},{4,3},{5,4},{6,5},{7,6},{8,7},{9,8},{10,9},{11,1... | collective-permute-start | bytes 147464 | tf_op jit(solution)/shard_map/ppermute | solution.py:28
  31.5 8.6 %collective-permute-start.3 = (f32[3,16,256]{2,1,0:T(8,128)S(1)}, f32[3,16,256]{2,1,0:T(8,128)S(1)}, u32[]{:S(2)}, u32[]{:S(2)}) collective-permute-start(f32[3,16,256]{2,1,0:T(8,128)S(1)} %pad_maximum_fusion.4), channel_id=1, source_target_pairs={{0,1},{1,2},{2,3},{3,4},{4,5},{5,6},{6,7},{7,8},{8,9},{9,10},{10,1... | collective-permute-start | bytes 147464 | tf_op jit(solution)/shard_map/ppermute | solution.py:28
  34.9 6.8 %collective-permute-start.4 = (f32[3,16,256]{2,1,0:T(8,128)S(1)}, f32[3,16,256]{2,1,0:T(8,128)S(1)}, u32[]{:S(2)}, u32[]{:S(2)}) collective-permute-start(f32[3,16,256]{2,1,0:T(8,128)S(1)} %pad_maximum_fusion.4), channel_id=1, source_target_pairs={{1,0},{2,1},{3,2},{4,3},{5,4},{6,5},{7,6},{8,7},{9,8},{10,9},{11,1... | collective-permute-start | bytes 147464 | tf_op jit(solution)/shard_map/ppermute | solution.py:28
  41.7 8.4 %collective-permute-start.5 = (f32[3,16,256]{2,1,0:T(8,128)S(1)}, f32[3,16,256]{2,1,0:T(8,128)S(1)}, u32[]{:S(2)}, u32[]{:S(2)}) collective-permute-start(f32[3,16,256]{2,1,0:T(8,128)S(1)} %pad_maximum_fusion.5), channel_id=1, source_target_pairs={{0,2},{1,3},{2,4},{3,5},{4,6},{5,7},{6,8},{7,9},{8,10},{9,11},{10,... | collective-permute-start | bytes 147464 | tf_op jit(solution)/shard_map/ppermute | solution.py:28
  47.9 7.5 %collective-permute-start.6 = (f32[3,16,256]{2,1,0:T(8,128)S(1)}, f32[3,16,256]{2,1,0:T(8,128)S(1)}, u32[]{:S(2)}, u32[]{:S(2)}) collective-permute-start(f32[3,16,256]{2,1,0:T(8,128)S(1)} %pad_maximum_fusion.5), channel_id=1, source_target_pairs={{2,0},{3,1},{4,2},{5,3},{6,4},{7,5},{8,6},{9,7},{10,8},{11,9},{12,... | collective-permute-start | bytes 147464 | tf_op jit(solution)/shard_map/ppermute | solution.py:28
  55.4 6.0 %collective-permute-start.7 = (f32[3,16,256]{2,1,0:T(8,128)S(1)}, f32[3,16,256]{2,1,0:T(8,128)S(1)}, u32[]{:S(2)}, u32[]{:S(2)}) collective-permute-start(f32[3,16,256]{2,1,0:T(8,128)S(1)} %pad_maximum_fusion.6), channel_id=1, source_target_pairs={{0,4},{1,5},{2,6},{3,7},{4,8},{5,9},{6,10},{7,11},{8,12},{9,13},{1... | collective-permute-start | bytes 147464 | tf_op jit(solution)/shard_map/ppermute | solution.py:28
  59.3 7.1 %collective-permute-start.8 = (f32[3,16,256]{2,1,0:T(8,128)S(1)}, f32[3,16,256]{2,1,0:T(8,128)S(1)}, u32[]{:S(2)}, u32[]{:S(2)}) collective-permute-start(f32[3,16,256]{2,1,0:T(8,128)S(1)} %pad_maximum_fusion.6), channel_id=1, source_target_pairs={{4,0},{5,1},{6,2},{7,3},{8,4},{9,5},{10,6},{11,7},{12,8},{13,9},{1... | collective-permute-start | bytes 147464 | tf_op jit(solution)/shard_map/ppermute | solution.py:28
  66.4 8.2 %collective-permute-start.9 = (f32[3,16,256]{2,1,0:T(8,128)S(1)}, f32[3,16,256]{2,1,0:T(8,128)S(1)}, u32[]{:S(2)}, u32[]{:S(2)}) collective-permute-start(f32[3,16,256]{2,1,0:T(8,128)S(1)} %pad_maximum_fusion.7), channel_id=1, source_target_pairs={{0,8},{1,9},{2,10},{3,11},{4,12},{5,13},{6,14},{7,15},{8,16},{9,17... | collective-permute-start | bytes 147464 | tf_op jit(solution)/shard_map/ppermute | solution.py:28
  72.9 6.9 %collective-permute-start.10 = (f32[3,16,256]{2,1,0:T(8,128)S(1)}, f32[3,16,256]{2,1,0:T(8,128)S(1)}, u32[]{:S(2)}, u32[]{:S(2)}) collective-permute-start(f32[3,16,256]{2,1,0:T(8,128)S(1)} %pad_maximum_fusion.7), channel_id=1, source_target_pairs={{8,0},{9,1},{10,2},{11,3},{12,4},{13,5},{14,6},{15,7},{16,8},{17,9... | collective-permute-start | bytes 147464 | tf_op jit(solution)/shard_map/ppermute | solution.py:28
  79.9 4.4 %collective-permute-start.11 = (f32[3,16,256]{2,1,0:T(8,128)S(1)}, f32[3,16,256]{2,1,0:T(8,128)S(1)}, u32[]{:S(2)}, u32[]{:S(2)}) collective-permute-start(f32[3,16,256]{2,1,0:T(8,128)S(1)} %pad_maximum_fusion.8), channel_id=1, source_target_pairs={{0,16},{1,17},{2,18},{3,19},{4,20},{5,21},{6,22},{7,23},{8,24},{9,... | collective-permute-start | bytes 147464 | tf_op jit(solution)/shard_map/ppermute | solution.py:28
  82.4 10.2 %collective-permute-start.12 = (f32[3,16,256]{2,1,0:T(8,128)S(1)}, f32[3,16,256]{2,1,0:T(8,128)S(1)}, u32[]{:S(2)}, u32[]{:S(2)}) collective-permute-start(f32[3,16,256]{2,1,0:T(8,128)S(1)} %pad_maximum_fusion.8), channel_id=1, source_target_pairs={{16,0},{17,1},{18,2},{19,3},{20,4},{21,5},{22,6},{23,7},{24,8},{25... | collective-permute-start | bytes 147464 | tf_op jit(solution)/shard_map/ppermute | solution.py:28
  92.6 7.7 %collective-permute-start.13 = (f32[16,256]{1,0:T(8,128)S(1)}, f32[16,256]{1,0:T(8,128)S(1)}, u32[]{:S(2)}, u32[]{:S(2)}) collective-permute-start(f32[16,256]{1,0:T(8,128)S(1)} %fusion.36), channel_id=1, source_target_pairs={{0,1},{1,2},{2,3},{3,4},{4,5},{5,6},{6,7},{7,8},{8,9},{9,10},{10,1... | collective-permute-start | bytes 49160 | tf_op jit(solution)/shard_map/ppermute | solution.py:28
where the time goes:
time: 102 us; the launch traced here: 101 us
  starting transfers between devices  46.3 us (45%)
  waiting for transfers between devices  33 us (32%)
  other arithmetic  15.6 us (15%)
  local copies, waits for them, and re-layouts  5.92 us (6%)
    ppermute x12, starting transfers between devices, from_behind(): return lax.ppermute(array, axis, pairs)  42 us
    ppermute x12, waiting for transfers between devices, from_behind(): return lax.ppermute(array, axis, pairs)  33 us
    div x5, other arithmetic, reduce_rows(): ratio_rhs = right_hand / main_band  3.6 us
    neg x1, other arithmetic, on_device(): high_all = -higher_coupling  3.46 us
    mul x1, other arithmetic, on_device(): transverse_speed * void_share  3.32 us
    ppermute x1, starting transfers between devices, extended(): lax.ppermute(lax.slice_in_dim(block, block.shape[dim] - width, None, axis...  2.41 us
    slice x12, local copies, waits for them, and re-layouts, from_earlier(): values[:-stride]  2.38 us
  transfers between devices with their start and end apart: 14, of which 12 were waited for; matrix products, arithmetic and copies ran while one was open for 6% of the time, Pallas kernels for 0%

commit v1 on v0

v1 whole, which is shorter than its diff:
```python
import functools

import jax
import jax.numpy as jnp
from jax import lax
from jax.experimental import pallas as pl
from jax.experimental.pallas import tpu as pltpu
from jax.sharding import PartitionSpec as P

transverse_speed = 0.35
mixing_coefficient = 0.15
supplied_power = 0.5
axial_drift = 64.0

MESH = pl.DeviceIdType.MESH
LANES = 128
RING_Y = 4


def spread(ref, value):
    for a in range(2):
        for b in range(2):
            ref[pl.ds(8 * (2 * a + b), 8), :] = value[8 * a : 8 * a + 8, LANES * b : LANES * (b + 1)]


def gathered(ref):
    parts = [ref[pl.ds(8 * t, 8), :] for t in range(4)]
    return jnp.concatenate(
        [jnp.concatenate(parts[:2], axis=1), jnp.concatenate(parts[2:], axis=1)], axis=0
    )


def kernel(
    axial,
    rows,
    layers,
    first_layer,
    depth,
    warmth_hbm,
    supply_hbm,
    lower_hbm,
    higher_hbm,
    ratio_hbm,
    group_hbm,
    region_hbm,
    sense_hbm,
    out_ref,
    warmth,
    supply,
    lower,
    higher,
    group,
    ratio,
    region,
    sense,
    gain,
    scale,
    low_scale,
    below,
    above,
    unit,
    rhs,
    halo_out,
    halo_low,
    halo_high,
    mat_out,
    mat_in,
    rhs_out,
    rhs_in,
    edge_out,
    edge_in,
    alpha,
    beta,
    load_sem,
    small_sem,
    own_sem,
    send_sem,
    recv_sem,
):
    me = lax.axis_index("axial")
    row = lax.axis_index("row")
    layer_count = axial // RING_Y
    solvers = layers * RING_Y
    g_size = axial // solvers
    my_layer = lax.rem(me // RING_Y - first_layer + layer_count, layer_count)
    my_solver = my_layer * RING_Y + lax.rem(me, RING_Y)
    solving = my_layer < layers
    has_low = row > 0
    has_high = row < rows - 1

    def device_of(s):
        return lax.rem(s // RING_Y + first_layer, layer_count) * RING_Y + lax.rem(s, RING_Y)

    barrier = pltpu.get_barrier_semaphore()

    @pl.when(has_low)
    def _():
        pl.semaphore_signal(barrier, inc=1, device_id=(row - 1, me), device_id_type=MESH)

    @pl.when(has_high)
    def _():
        pl.semaphore_signal(barrier, inc=1, device_id=(row + 1, me), device_id_type=MESH)

    def greet(j, carry):
        @pl.when(j != me)
        def _():
            pl.semaphore_signal(barrier, inc=1, device_id=(row, j), device_id_type=MESH)

        return carry

    def greet_solver(s, carry):
        return greet(device_of(s), carry)

    if layers == layer_count:
        lax.fori_loop(0, axial, greet, 0)
    else:

        @pl.when(solving)
        def _():
            lax.fori_loop(0, axial, greet, 0)

        @pl.when(jnp.logical_not(solving))
        def _():
            lax.fori_loop(0, solvers, greet_solver, 0)

    loads = [
        pltpu.make_async_copy(source, target, load_sem.at[i])
        for i, (source, target) in enumerate(
            [
                (warmth_hbm, warmth),
                (higher_hbm, higher),
                (lower_hbm, lower),
                (supply_hbm, supply),
                (group_hbm, group),
            ]
        )
    ]
    smalls = [
        pltpu.make_async_copy(source, target, small_sem.at[i])
        for i, (source, target) in enumerate(
            [(ratio_hbm, ratio), (region_hbm, region), (sense_hbm, sense)]
        )
    ]
    for copy in loads + smalls:
        copy.start()

    loads[0].wait()
    for z in range(depth):
        halo_out[0, pl.ds(z, 1), :] = warmth[pl.ds(16 * z, 1), :]
        halo_out[1, pl.ds(z, 1), :] = warmth[pl.ds(16 * z + 15, 1), :]

    others = jnp.where(solving, axial - 1, solvers)
    pl.semaphore_wait(barrier, others + has_low.astype(jnp.int32) + has_high.astype(jnp.int32))

    to_low = functools.partial(
        pltpu.make_async_remote_copy,
        halo_out.at[0],
        halo_high,
        send_sem.at[0],
        recv_sem.at[0],
        device_id_type=MESH,
    )
    to_high = functools.partial(
        pltpu.make_async_remote_copy,
        halo_out.at[1],
        halo_low,
        send_sem.at[1],
        recv_sem.at[1],
        device_id_type=MESH,
    )

    @pl.when(has_low)
    def _():
        to_low(device_id=(row - 1, me)).start()

    @pl.when(has_high)
    def _():
        to_high(device_id=(row + 1, me)).start()

    @pl.when(jnp.logical_not(has_low))
    def _():
        halo_low[...] = jnp.zeros_like(halo_low)

    @pl.when(jnp.logical_not(has_high))
    def _():
        halo_high[...] = jnp.zeros_like(halo_high)

    def slab(z):
        return pl.ds(16 * z, 16)

    loads[1].wait()
    loads[2].wait()
    kept = jnp.ones((16, 256), jnp.float32)
    weight = jnp.ones((16, 256), jnp.float32)
    source = jnp.zeros((16, 256), jnp.float32)
    last = depth - 1
    for z in range(last):
        low = lower[slab(z), :] + axial_drift
        high = higher[slab(z), :]
        excess = 1.0 + low * kept
        inverse = 1.0 / (excess + high)
        low_ratio = low * inverse
        gain[slab(z), :] = high * inverse
        scale[slab(z), :] = inverse
        low_scale[slab(z), :] = low_ratio
        kept = excess * inverse
        weight = low_ratio * weight
        source = inverse + low_ratio * source
        below[slab(z), :] = weight
        unit[slab(z), :] = source
    low_last = lower[slab(last), :] + axial_drift
    inverse_high = 1.0 / higher[slab(last), :]
    spread(mat_out.at[0], low_last * weight * inverse_high)
    spread(mat_out.at[1], (1.0 + low_last * source) * inverse_high)
    reach_low = weight
    reach_high = gain[slab(last - 1), :]
    response = source
    above[slab(last - 1), :] = reach_high
    for z in reversed(range(last - 1)):
        factor = gain[slab(z), :]
        reach_high = factor * reach_high
        reach_low = below[slab(z), :] + factor * reach_low
        response = unit[slab(z), :] + factor * response
        above[slab(z), :] = reach_high
        below[slab(z), :] = reach_low
    spread(mat_out.at[2], response)
    spread(mat_out.at[3], reach_high)

    def scatter(out, into, which):
        own = pltpu.make_async_copy(
            out.at[:, pl.ds(my_solver * g_size, g_size)],
            into.at[:, pl.ds(me * g_size, g_size)],
            own_sem.at[which],
        )

        def send(s, carry):
            target = device_of(s)

            @pl.when(target != me)
            def _():
                pltpu.make_async_remote_copy(
                    out.at[:, pl.ds(s * g_size, g_size)],
                    into.at[:, pl.ds(me * g_size, g_size)],
                    send_sem.at[2 + which],
                    recv_sem.at[2 + which],
                    device_id=(row, target),
                    device_id_type=MESH,
                ).start()

            return carry

        lax.fori_loop(0, solvers, send, 0)

        @pl.when(solving)
        def _():
            own.start()

        return own

    def drain(ref, sem, count):
        part = ref.at[:, pl.ds(0, count)]
        pltpu.make_async_copy(part, part, sem).wait()

    own_matrix = scatter(mat_out, mat_in, 0)

    for copy in [loads[3], loads[4]] + smalls:
        copy.wait()
    kind = group[...]
    share = jnp.zeros((16, 256), jnp.float32)
    for c in range(ratio.shape[0]):
        share = jnp.where(kind == c, transverse_speed * ratio[c], share)
    row_at = lax.broadcasted_iota(jnp.int32, (16, 256), 0)
    lane_at = lax.broadcasted_iota(jnp.int32, (16, 256), 1)
    centre = (1.0 - 4.0 * mixing_coefficient) - share
    share_low = jnp.where(row_at == 0, 0.0, share)
    mixing_low = jnp.where(row_at == 0, 0.0, mixing_coefficient)
    share_high = jnp.where(row_at == 15, 0.0, share)
    mixing_high = jnp.where(row_at == 15, 0.0, mixing_coefficient)
    mixing_left = jnp.where(lane_at == 0, 0.0, mixing_coefficient)
    mixing_right = jnp.where(lane_at == 255, 0.0, mixing_coefficient)

    def direction(z):
        return sense[region[z]].astype(jnp.float32)

    for z in range(depth):
        forward = direction(z)
        here = warmth[slab(z), :]
        rhs[slab(z), :] = (
            centre * here
            + (mixing_low + forward * share_low) * pltpu.roll(here, 1, 0)
            + (mixing_high + (1.0 - forward) * share_high) * pltpu.roll(here, 15, 0)
            + mixing_left * pltpu.roll(here, 1, 1)
            + mixing_right * pltpu.roll(here, 255, 1)
            + supplied_power * supply[slab(z), :]
        )

    @pl.when(has_high)
    def _():
        to_low(device_id=(row, me)).wait_recv()

    @pl.when(has_low)
    def _():
        to_high(device_id=(row, me)).wait_recv()

    edge_share_low = share[0:8, :] - share_low[0:8, :]
    edge_mixing_low = mixing_coefficient - mixing_low[0:8, :]
    edge_share_high = share[8:16, :] - share_high[8:16, :]
    edge_mixing_high = mixing_coefficient - mixing_high[8:16, :]

    def whole_rhs(z):
        forward = direction(z)
        low_row = (edge_mixing_low + forward * edge_share_low) * halo_low[pl.ds(z, 1), :]
        high_row = (edge_mixing_high + (1.0 - forward) * edge_share_high) * halo_high[pl.ds(z, 1), :]
        return rhs[slab(z), :] + jnp.concatenate([low_row, high_row], axis=0)

    value = jnp.zeros((16, 256), jnp.float32)
    for z in range(last):
        value = scale[slab(z), :] * whole_rhs(z) + low_scale[slab(z), :] * value
        rhs[slab(z), :] = value
    spread(rhs_out.at[0], (whole_rhs(last) + low_last * value) * inverse_high)
    for z in reversed(range(last - 1)):
        value = rhs[slab(z), :] + gain[slab(z), :] * value
        rhs[slab(z), :] = value
    spread(rhs_out.at[1], value)
    own_rhs = scatter(rhs_out, rhs_in, 1)

    lines = axial * g_size
    own_back = pltpu.make_async_copy(
        edge_out.at[:, pl.ds(me * g_size, g_size)],
        edge_in.at[:, pl.ds(my_solver * g_size, g_size)],
        own_sem.at[2],
    )

    @pl.when(solving)
    def _():
        at = lax.broadcasted_iota(jnp.int32, (lines, LANES), 0)

        def down(x, blocks):
            return pltpu.roll(x, blocks * g_size, 0)

        def up(x, blocks):
            return pltpu.roll(x, lines - blocks * g_size, 0)

        is_first = at < g_size
        is_last = at >= lines - g_size
        drain(mat_in, recv_sem.at[2], (axial - 1) * g_size)
        own_matrix.wait()
        low = mat_in[0]
        excess = mat_in[1] + jnp.where(is_last, 1.0, up(mat_in[2], 1))
        high = jnp.where(is_last, 0.0, up(mat_in[3], 1))
        excess = jnp.where(is_first, excess + low, excess)
        low = jnp.where(is_first, 0.0, low)
        level, stride = 0, 1
        while stride < axial:
            inverse = 1.0 / (low + excess + high)
            a = low * down(inverse, stride)
            b = high * up(inverse, stride)
            alpha[level] = a
            beta[level] = b
            excess = excess + a * down(excess, stride) + b * up(excess, stride)
            low = a * down(low, stride)
            high = b * up(high, stride)
            level, stride = level + 1, stride * 2
        final = 1.0 / excess

        drain(rhs_in, recv_sem.at[3], (axial - 1) * g_size)
        own_rhs.wait()
        r = rhs_in[0] + jnp.where(is_last, 0.0, up(rhs_in[1], 1))
        level, stride = 0, 1
        while stride < axial:
            r = r + alpha[level] * down(r, stride) + beta[level] * up(r, stride)
            level, stride = level + 1, stride * 2
        r = r * final
        edge_out[1] = r
        edge_out[0] = jnp.where(is_first, 0.0, down(r, 1))

        def send(j, carry):
            @pl.when(j != me)
            def _():
                pltpu.make_async_remote_copy(
                    edge_out.at[:, pl.ds(j * g_size, g_size)],
                    edge_in.at[:, pl.ds(my_solver * g_size, g_size)],
                    send_sem.at[4],
                    recv_sem.at[4],
                    device_id=(row, j),
                    device_id_type=MESH,
                ).start()

            return carry

        lax.fori_loop(0, axial, send, 0)
        own_back.start()
        own_back.wait()
        drain(edge_in, recv_sem.at[4], axial - g_size)

    if layers != layer_count:

        @pl.when(jnp.logical_not(solving))
        def _():
            drain(edge_in, recv_sem.at[4], axial)

    below_edge = gathered(edge_in.at[0])
    own_edge = gathered(edge_in.at[1])
    for z in range(last):
        out_ref[slab(z), :] = (
            rhs[slab(z), :] + below[slab(z), :] * below_edge + above[slab(z), :] * own_edge
        )
    out_ref[slab(last), :] = own_edge

    @pl.when(has_low)
    def _():
        to_low(device_id=(row, me)).wait_send()

    @pl.when(has_high)
    def _():
        to_high(device_id=(row, me)).wait_send()

    @pl.when(solving)
    def _():
        drain(mat_out, send_sem.at[2], axial - g_size)
        drain(rhs_out, send_sem.at[3], axial - g_size)
        drain(edge_out, send_sem.at[4], (axial - 1) * g_size)

    if layers != layer_count:

        @pl.when(jnp.logical_not(solving))
        def _():
            drain(mat_out, send_sem.at[2], axial)
            drain(rhs_out, send_sem.at[3], axial)


def solution(mesh):
    axial, rows = mesh.shape["axial"], mesh.shape["row"]
    layer_count = axial // RING_Y
    layers, first_layer = layer_count, 0

    def on_device(warmth, supply, lower, higher, ratio, group, region, sense):
        depth, width, length = warmth.shape
        flat = (depth * width, length)
        lines = axial * (layer_count // layers)
        levels = axial.bit_length() - 1
        field = pltpu.VMEM(flat, jnp.float32)
        halo = pltpu.VMEM((depth, length), jnp.float32)
        out = pl.pallas_call(
            functools.partial(kernel, axial, rows, layers, first_layer, depth),
            out_shape=jax.ShapeDtypeStruct(flat, jnp.float32),
            in_specs=[pl.BlockSpec(memory_space=pl.ANY)] * 8,
            out_specs=pl.BlockSpec(memory_space=pltpu.VMEM),
            scratch_shapes=[
                field,
                field,
                field,
                field,
                pltpu.VMEM(group.shape, jnp.int32),
                pltpu.SMEM(ratio.shape, jnp.float32),
                pltpu.SMEM(region.shape, jnp.int32),
                pltpu.SMEM(sense.shape, jnp.int32),
                field,
                field,
                field,
                field,
                field,
                field,
                field,
                pltpu.VMEM((2, depth, length), jnp.float32),
                halo,
                halo,
                pltpu.VMEM((4, axial, LANES), jnp.float32),
                pltpu.VMEM((4, lines, LANES), jnp.float32),
                pltpu.VMEM((2, axial, LANES), jnp.float32),
                pltpu.VMEM((2, lines, LANES), jnp.float32),
                pltpu.VMEM((2, lines, LANES), jnp.float32),
                pltpu.VMEM((2, axial, LANES), jnp.float32),
                pltpu.VMEM((levels, lines, LANES), jnp.float32),
                pltpu.VMEM((levels, lines, LANES), jnp.float32),
                pltpu.SemaphoreType.DMA((5,)),
                pltpu.SemaphoreType.DMA((3,)),
                pltpu.SemaphoreType.DMA((3,)),
                pltpu.SemaphoreType.DMA((5,)),
                pltpu.SemaphoreType.DMA((5,)),
            ],
            compiler_params=pltpu.CompilerParams(
                collective_id=0, has_side_effects=True, vmem_limit_bytes=32 * 1024 * 1024
            ),
        )(
            warmth.reshape(flat),
            supply.reshape(flat),
            lower.reshape(flat),
            higher.reshape(flat),
            ratio,
            group,
            region,
            sense,
        )
        return out.reshape(warmth.shape)

    placed = (
        P("axial", "row", None),
        P("axial", "row", None),
        P("axial", "row", None),
        P("axial", "row", None),
        P(),
        P("row", None),
        P("axial"),
        P(),
    )
    return jax.shard_map(
        on_device, mesh=mesh, in_specs=placed, out_specs=P("axial", "row", None), check_vma=False
    )
```

time: 102 us -> 31.7 us (0.31)
  the two profiles are of different devices: /device:TPU:36 before, /device:TPU:1 now
where the time goes in v1:
time: 31.7 us; the launch traced here: 31.4 us
  Pallas kernels  25 us (79%)
  local copies, waits for them, and re-layouts  6.36 us (20%)
    pallas_call x1, Pallas kernels, on_device(): pl.pallas_call(functools.partial(kernel, axial, rows, layers, first_layer...  25 us
    unnamed x17, local copies, waits for them, and re-layouts  6.36 us

profile of v1, /device:TPU:1, one launch (start us, length us, event | category | flops | bytes accessed | tf_op | source)
XLA Modules:
  0.0 31.4 jit_solution(2081243474174985102)
XLA Ops:
  0.0 0.0 copy-start.5
  0.0 0.0 copy-start.6
  0.0 0.0 copy-start.7
  0.0 0.6 %copy-done.5 = f32[4]{0:T(128)S(1)} copy-done((f32[4]{0:T(128)S(1)}, f32[4]{0:T(128)}, u32[]{:S(2)}) %copy-start.5) | copy-done | bytes 40
  0.7 0.0 copy-done.6
  0.7 0.0 copy-done.7
  0.7 0.0 copy-start
  0.7 1.0 %copy-done = f32[32,16,256]{2,1,0:T(8,128)S(1)} copy-done((f32[32,16,256]{2,1,0:T(8,128)S(1)}, f32[32,16,256]{2,1,0:T(8,128)}, u32[]{:S(2)}) %copy-start) | copy-done | bytes 524312
  1.7 0.0 copy-start.1
  1.7 1.0 %copy-done.1 = f32[32,16,256]{2,1,0:T(8,128)S(1)} copy-done((f32[32,16,256]{2,1,0:T(8,128)S(1)}, f32[32,16,256]{2,1,0:T(8,128)}, u32[]{:S(2)}) %copy-start.1) | copy-done | bytes 524312
  2.8 0.0 copy-start.2
  2.8 1.0 %copy-done.2 = f32[32,16,256]{2,1,0:T(8,128)S(1)} copy-done((f32[32,16,256]{2,1,0:T(8,128)S(1)}, f32[32,16,256]{2,1,0:T(8,128)}, u32[]{:S(2)}) %copy-start.2) | copy-done | bytes 524312
  3.8 0.0 copy-start.3
  3.8 1.0 %copy-done.3 = f32[32,16,256]{2,1,0:T(8,128)S(1)} copy-done((f32[32,16,256]{2,1,0:T(8,128)S(1)}, f32[32,16,256]{2,1,0:T(8,128)}, u32[]{:S(2)}) %copy-start.3) | copy-done | bytes 524312
  4.9 0.0 copy-start.4
  4.9 0.7 %copy-done.4 = s32[16,256]{1,0:T(8,128)S(1)} copy-done((s32[16,256]{1,0:T(8,128)S(1)}, s32[16,256]{1,0:T(8,128)}, u32[]{:S(2)}) %copy-start.4) | copy-done | bytes 16408
  5.6 25.0 %shard_map.82 = f32[512,256]{1,0:T(8,128)S(1)} custom-call(f32[512,256]{1,0:T(8,128)S(1)} %bitcast.6, f32[512,256]{1,0:T(8,128)S(1)} %bitcast.7, f32[512,256]{1,0:T(8,128)S(1)} %bitcast.8, f32[512,256]{1,0:T(8,128)S(1)} %bitcast.9, f32[4]{0:T(128)S(1)} %copy-done.5, s32[16,256]{1,0:T(8,128)S(1)} %copy-done.4, s32[32]{0:T(128)S(1)} %copy-done.6, s32[32]{0:T(128)S(1)} %copy-done.7), custom_call_target="tpu_custom_call" | custom-call | tf_op jit(solution)/shard_map/pallas_call | solution.py:444
  30.6 0.8 %copy.10 = f32[32,16,256]{2,1,0:T(8,128)} copy(f32[32,16,256]{2,1,0:T(8,128)S(1)} %bitcast.5) | data formatting | bytes 1048576
Async XLA Ops:
  0.0 0.7 %copy-start.5 = (f32[4]{0:T(128)S(1)}, f32[4]{0:T(128)}, u32[]{:S(2)}) copy-start(f32[4]{0:T(128)} %ratio_hbm.1) | copy-start | bytes 52
  0.0 0.7 %copy-start.6 = (s32[32]{0:T(128)S(1)}, s32[32]{0:T(128)}, u32[]{:S(2)}) copy-start(s32[32]{0:T(128)} %region_hbm.1) | copy-start | bytes 388
  0.0 0.7 %copy-start.7 = (s32[32]{0:T(128)S(1)}, s32[32]{0:T(128)}, u32[]{:S(2)}) copy-start(s32[32]{0:T(128)} %sense_hbm.1) | copy-start | bytes 388
  0.7 1.0 %copy-start = (f32[32,16,256]{2,1,0:T(8,128)S(1)}, f32[32,16,256]{2,1,0:T(8,128)}, u32[]{:S(2)}) copy-start(f32[32,16,256]{2,1,0:T(8,128)} %param.8) | copy-start | bytes 1572868
  1.7 1.0 %copy-start.1 = (f32[32,16,256]{2,1,0:T(8,128)S(1)}, f32[32,16,256]{2,1,0:T(8,128)}, u32[]{:S(2)}) copy-start(f32[32,16,256]{2,1,0:T(8,128)} %param.9) | copy-start | bytes 1572868
  2.8 1.0 %copy-start.2 = (f32[32,16,256]{2,1,0:T(8,128)S(1)}, f32[32,16,256]{2,1,0:T(8,128)}, u32[]{:S(2)}) copy-start(f32[32,16,256]{2,1,0:T(8,128)} %param.10) | copy-start | bytes 1572868
  3.8 1.0 %copy-start.3 = (f32[32,16,256]{2,1,0:T(8,128)S(1)}, f32[32,16,256]{2,1,0:T(8,128)}, u32[]{:S(2)}) copy-start(f32[32,16,256]{2,1,0:T(8,128)} %param.11) | copy-start | bytes 1572868
  4.9 0.7 %copy-start.4 = (s32[16,256]{1,0:T(8,128)S(1)}, s32[16,256]{1,0:T(8,128)}, u32[]{:S(2)}) copy-start(s32[16,256]{1,0:T(8,128)} %group_hbm.1) | copy-start | bytes 49156

commit v2 on v1

--- a/solution.py
+++ b/solution.py
@@ -108,20 +108,9 @@
 
         return carry
 
-    def greet_solver(s, carry):
-        return greet(device_of(s), carry)
-
-    if layers == layer_count:
+    @pl.when(solving)
+    def _():
         lax.fori_loop(0, axial, greet, 0)
-    else:
-
-        @pl.when(solving)
-        def _():
-            lax.fori_loop(0, axial, greet, 0)
-
-        @pl.when(jnp.logical_not(solving))
-        def _():
-            lax.fori_loop(0, solvers, greet_solver, 0)
 
     loads = [
         pltpu.make_async_copy(source, target, load_sem.at[i])
@@ -149,7 +138,7 @@
         halo_out[0, pl.ds(z, 1), :] = warmth[pl.ds(16 * z, 1), :]
         halo_out[1, pl.ds(z, 1), :] = warmth[pl.ds(16 * z + 15, 1), :]
 
-    others = jnp.where(solving, axial - 1, solvers)
+    others = jnp.where(solving, solvers - 1, solvers)
     pl.semaphore_wait(barrier, others + has_low.astype(jnp.int32) + has_high.astype(jnp.int32))
 
     to_low = functools.partial(
@@ -432,7 +421,7 @@
 def solution(mesh):
     axial, rows = mesh.shape["axial"], mesh.shape["row"]
     layer_count = axial // RING_Y
-    layers, first_layer = layer_count, 0
+    layers, first_layer = 2, 0
 
     def on_device(warmth, supply, lower, higher, ratio, group, region, sense):
         depth, width, length = warmth.shape
@@ -444,7 +433,7 @@
         out = pl.pallas_call(
             functools.partial(kernel, axial, rows, layers, first_layer, depth),
             out_shape=jax.ShapeDtypeStruct(flat, jnp.float32),
-            in_specs=[pl.BlockSpec(memory_space=pl.ANY)] * 8,
+            in_specs=[pl.BlockSpec(memory_space=pltpu.HBM)] * 8,
             out_specs=pl.BlockSpec(memory_space=pltpu.VMEM),
             scratch_shapes=[
                 field,
@@ -483,14 +472,19 @@
                 collective_id=0, has_side_effects=True, vmem_limit_bytes=32 * 1024 * 1024
             ),
         )(
-            warmth.reshape(flat),
-            supply.reshape(flat),
-            lower.reshape(flat),
-            higher.reshape(flat),
-            ratio,
-            group,
-            region,
-            sense,
+            *(
+                pltpu.with_memory_space_constraint(x, pltpu.HBM)
+                for x in (
+                    warmth.reshape(flat),
+                    supply.reshape(flat),
+                    lower.reshape(flat),
+                    higher.reshape(flat),
+                    ratio,
+                    group,
+                    region,
+                    sense,
+                )
+            )
         )
         return out.reshape(warmth.shape)
 

time: 31.7 us -> 22.7 us (0.72)
  the two profiles are of different devices: /device:TPU:1 before, /device:TPU:2 now
where the time goes in v2:
time: 22.7 us; the launch traced here: 22.6 us
  Pallas kernels  21.8 us (96%)
  local copies, waits for them, and re-layouts  0.8 us (4%)
    pallas_call x1, Pallas kernels, on_device(): pl.pallas_call(functools.partial(kernel, axial, rows, layers, first_layer...  21.8 us
    unnamed x1, local copies, waits for them, and re-layouts  0.8 us

profile of v2, /device:TPU:2, one launch (start us, length us, event | category | flops | bytes accessed | tf_op | source)
XLA Modules:
  0.0 22.6 jit_solution(7749131384297792426)
XLA Ops:
  0.0 21.8 %shard_map.82 = f32[512,256]{1,0:T(8,128)S(1)} custom-call(f32[512,256]{1,0:T(8,128)} %bitcast.6, f32[512,256]{1,0:T(8,128)} %bitcast.7, f32[512,256]{1,0:T(8,128)} %bitcast.8, f32[512,256]{1,0:T(8,128)} %bitcast.9, f32[4]{0:T(128)} %ratio_hbm.1, s32[16,256]{1,0:T(8,128)} %group_hbm.1, s32[32]{0:T(128)} %region_hbm.1, s32[32]{0:T(128)} %sense_hbm.1), custom_call_target="tpu_custom_call" | custom-call | tf_op jit(solution)/shard_map/pallas_call | solution.py:433
  21.8 0.8 %copy.10 = f32[32,16,256]{2,1,0:T(8,128)} copy(f32[32,16,256]{2,1,0:T(8,128)S(1)} %bitcast.5) | data formatting | bytes 1048576

commit v3 on v2

--- a/solution.py
+++ b/solution.py
@@ -15,6 +15,7 @@
 MESH = pl.DeviceIdType.MESH
 LANES = 128
 RING_Y = 4
+LAYERS = 2
 
 
 def spread(ref, value):
@@ -33,7 +34,6 @@
 def kernel(
     axial,
     rows,
-    layers,
     first_layer,
     depth,
     warmth_hbm,
@@ -60,6 +60,7 @@
     above,
     unit,
     rhs,
+    part,
     halo_out,
     halo_low,
     halo_high,
@@ -69,8 +70,15 @@
     rhs_in,
     edge_out,
     edge_in,
+    side_rhs_out,
+    side_rhs_in,
+    side_edge_out,
+    side_edge_in,
     alpha,
     beta,
+    side_alpha,
+    side_beta,
+    finals,
     load_sem,
     small_sem,
     own_sem,
@@ -80,16 +88,22 @@
     me = lax.axis_index("axial")
     row = lax.axis_index("row")
     layer_count = axial // RING_Y
-    solvers = layers * RING_Y
+    solvers = LAYERS * RING_Y
     g_size = axial // solvers
+    my_y = lax.rem(me, RING_Y)
     my_layer = lax.rem(me // RING_Y - first_layer + layer_count, layer_count)
-    my_solver = my_layer * RING_Y + lax.rem(me, RING_Y)
-    solving = my_layer < layers
+    my_solver = 2 * my_y + lax.rem(my_layer + my_y // 2, 2)
+    solving = my_layer < LAYERS
+    siding = my_layer == 0
     has_low = row > 0
     has_high = row < rows - 1
 
     def device_of(s):
-        return lax.rem(s // RING_Y + first_layer, layer_count) * RING_Y + lax.rem(s, RING_Y)
+        layer = lax.rem(s + s // 4, 2)
+        return lax.rem(layer + first_layer, layer_count) * RING_Y + s // 2
+
+    def side_device(h):
+        return first_layer * RING_Y + h
 
     barrier = pltpu.get_barrier_semaphore()
 
@@ -110,15 +124,15 @@
 
     @pl.when(solving)
     def _():
-        lax.fori_loop(0, axial, greet, 0)
+        lax.fori_loop(0, axial, lambda i, c: greet(axial - 1 - i, c), 0)
 
     loads = [
         pltpu.make_async_copy(source, target, load_sem.at[i])
         for i, (source, target) in enumerate(
             [
-                (warmth_hbm, warmth),
                 (higher_hbm, higher),
                 (lower_hbm, lower),
+                (warmth_hbm, warmth),
                 (supply_hbm, supply),
                 (group_hbm, group),
             ]
@@ -133,52 +147,11 @@
     for copy in loads + smalls:
         copy.start()
 
-    loads[0].wait()
-    for z in range(depth):
-        halo_out[0, pl.ds(z, 1), :] = warmth[pl.ds(16 * z, 1), :]
-        halo_out[1, pl.ds(z, 1), :] = warmth[pl.ds(16 * z + 15, 1), :]
-
-    others = jnp.where(solving, solvers - 1, solvers)
-    pl.semaphore_wait(barrier, others + has_low.astype(jnp.int32) + has_high.astype(jnp.int32))
-
-    to_low = functools.partial(
-        pltpu.make_async_remote_copy,
-        halo_out.at[0],
-        halo_high,
-        send_sem.at[0],
-        recv_sem.at[0],
-        device_id_type=MESH,
-    )
-    to_high = functools.partial(
-        pltpu.make_async_remote_copy,
-        halo_out.at[1],
-        halo_low,
-        send_sem.at[1],
-        recv_sem.at[1],
-        device_id_type=MESH,
-    )
-
-    @pl.when(has_low)
-    def _():
-        to_low(device_id=(row - 1, me)).start()
-
-    @pl.when(has_high)
-    def _():
-        to_high(device_id=(row + 1, me)).start()
-
-    @pl.when(jnp.logical_not(has_low))
-    def _():
-        halo_low[...] = jnp.zeros_like(halo_low)
-
-    @pl.when(jnp.logical_not(has_high))
-    def _():
-        halo_high[...] = jnp.zeros_like(halo_high)
-
     def slab(z):
         return pl.ds(16 * z, 16)
 
+    loads[0].wait()
     loads[1].wait()
-    loads[2].wait()
     kept = jnp.ones((16, 256), jnp.float32)
     weight = jnp.ones((16, 256), jnp.float32)
     source = jnp.zeros((16, 256), jnp.float32)
@@ -215,6 +188,47 @@
     spread(mat_out.at[2], response)
     spread(mat_out.at[3], reach_high)
 
+    loads[2].wait()
+    for z in range(depth):
+        halo_out[0, pl.ds(z, 1), :] = warmth[pl.ds(16 * z, 1), :]
+        halo_out[1, pl.ds(z, 1), :] = warmth[pl.ds(16 * z + 15, 1), :]
+
+    others = jnp.where(solving, solvers - 1, solvers)
+    pl.semaphore_wait(barrier, others + has_low.astype(jnp.int32) + has_high.astype(jnp.int32))
+
+    to_low = functools.partial(
+        pltpu.make_async_remote_copy,
+        halo_out.at[0],
+        halo_high,
+        send_sem.at[0],
+        recv_sem.at[0],
+        device_id_type=MESH,
+    )
+    to_high = functools.partial(
+        pltpu.make_async_remote_copy,
+        halo_out.at[1],
+        halo_low,
+        send_sem.at[1],
+        recv_sem.at[1],
+        device_id_type=MESH,
+    )
+
+    @pl.when(has_low)
+    def _():
+        to_low(device_id=(row - 1, me)).start()
+
+    @pl.when(has_high)
+    def _():
+        to_high(device_id=(row + 1, me)).start()
+
+    @pl.when(jnp.logical_not(has_low))
+    def _():
+        halo_low[...] = jnp.zeros_like(halo_low)
+
+    @pl.when(jnp.logical_not(has_high))
+    def _():
+        halo_high[...] = jnp.zeros_like(halo_high)
+
     def scatter(out, into, which):
         own = pltpu.make_async_copy(
             out.at[:, pl.ds(my_solver * g_size, g_size)],
@@ -283,6 +297,17 @@
             + supplied_power * supply[slab(z), :]
         )
 
+    first_value = scale[slab(0), :] * rhs[slab(0), :]
+    value = first_value
+    for z in range(1, last):
+        value = scale[slab(z), :] * rhs[slab(z), :] + low_scale[slab(z), :] * value
+        part[slab(z), :] = value
+    spread(rhs_out.at[0], (rhs[slab(last), :] + low_last * value) * inverse_high)
+    for z in reversed(range(1, last - 1)):
+        value = part[slab(z), :] + gain[slab(z), :] * value
+    spread(rhs_out.at[1], first_value + gain[slab(0), :] * value)
+    own_rhs = scatter(rhs_out, rhs_in, 1)
+
     @pl.when(has_high)
     def _():
         to_low(device_id=(row, me)).wait_recv()
@@ -302,18 +327,61 @@
         high_row = (edge_mixing_high + (1.0 - forward) * edge_share_high) * halo_high[pl.ds(z, 1), :]
         return rhs[slab(z), :] + jnp.concatenate([low_row, high_row], axis=0)
 
+    def sides(ref, value):
+        for h in range(4):
+            x, half = 15 * (h // 2), LANES * (h % 2)
+            ref[pl.ds(h, 1), :] = value[x : x + 1, half : half + LANES]
+
     value = jnp.zeros((16, 256), jnp.float32)
     for z in range(last):
         value = scale[slab(z), :] * whole_rhs(z) + low_scale[slab(z), :] * value
         rhs[slab(z), :] = value
-    spread(rhs_out.at[0], (whole_rhs(last) + low_last * value) * inverse_high)
+    sides(side_rhs_out.at[0], (whole_rhs(last) + low_last * value) * inverse_high)
     for z in reversed(range(last - 1)):
         value = rhs[slab(z), :] + gain[slab(z), :] * value
         rhs[slab(z), :] = value
-    spread(rhs_out.at[1], value)
-    own_rhs = scatter(rhs_out, rhs_in, 1)
+    sides(side_rhs_out.at[1], value)
+    own_side = pltpu.make_async_copy(
+        side_rhs_out.at[:, pl.ds(my_y, 1)], side_rhs_in.at[:, pl.ds(me, 1)], own_sem.at[3]
+    )
+
+    def send_side(h, carry):
+        target = side_device(h)
+
+        @pl.when(target != me)
+        def _():
+            pltpu.make_async_remote_copy(
+                side_rhs_out.at[:, pl.ds(h, 1)],
+                side_rhs_in.at[:, pl.ds(me, 1)],
+                send_sem.at[5],
+                recv_sem.at[5],
+                device_id=(row, target),
+                device_id_type=MESH,
+            ).start()
+
+        return carry
+
+    lax.fori_loop(0, RING_Y, send_side, 0)
+
+    @pl.when(siding)
+    def _():
+        own_side.start()
 
     lines = axial * g_size
+    def send_back(j, carry):
+        @pl.when(j != me)
+        def _():
+            pltpu.make_async_remote_copy(
+                edge_out.at[:, pl.ds(j * g_size, g_size)],
+                edge_in.at[:, pl.ds(my_solver * g_size, g_size)],
+                send_sem.at[4],
+                recv_sem.at[4],
+                device_id=(row, j),
+                device_id_type=MESH,
+            ).start()
+
+        return carry
+
     own_back = pltpu.make_async_copy(
         edge_out.at[:, pl.ds(me * g_size, g_size)],
         edge_in.at[:, pl.ds(my_solver * g_size, g_size)],
@@ -351,6 +419,7 @@
             high = b * up(high, stride)
             level, stride = level + 1, stride * 2
         final = 1.0 / excess
+        finals[...] = final
 
         drain(rhs_in, recv_sem.at[3], (axial - 1) * g_size)
         own_rhs.wait()
@@ -363,14 +432,48 @@
         edge_out[1] = r
         edge_out[0] = jnp.where(is_first, 0.0, down(r, 1))
 
+        lax.fori_loop(0, 4, send_back, 0)
+        own_back.start()
+
+    own_side_back = pltpu.make_async_copy(
+        side_edge_out.at[:, pl.ds(me, 1)], side_edge_in.at[:, pl.ds(my_y, 1)], own_sem.at[4]
+    )
+
+    @pl.when(siding)
+    def _():
+        at = lax.broadcasted_iota(jnp.int32, (axial, LANES), 0)
+
+        def down(x, blocks):
+            return pltpu.roll(x, blocks, 0)
+
+        def up(x, blocks):
+            return pltpu.roll(x, axial - blocks, 0)
+
+        local = 3 * (my_y // 2)
+        levels = alpha.shape[0]
+        for level in range(levels):
+            side_alpha[level] = alpha[level, pl.ds(local, axial, stride=g_size), :]
+            side_beta[level] = beta[level, pl.ds(local, axial, stride=g_size), :]
+        final = finals[pl.ds(local, axial, stride=g_size), :]
+        drain(side_rhs_in, recv_sem.at[5], axial - 1)
+        own_side.wait()
+        r = side_rhs_in[0] + jnp.where(at == axial - 1, 0.0, up(side_rhs_in[1], 1))
+        level, stride = 0, 1
+        while stride < axial:
+            r = r + side_alpha[level] * down(r, stride) + side_beta[level] * up(r, stride)
+            level, stride = level + 1, stride * 2
+        r = r * final
+        side_edge_out[1] = r
+        side_edge_out[0] = jnp.where(at == 0, 0.0, down(r, 1))
+
         def send(j, carry):
             @pl.when(j != me)
             def _():
                 pltpu.make_async_remote_copy(
-                    edge_out.at[:, pl.ds(j * g_size, g_size)],
-                    edge_in.at[:, pl.ds(my_solver * g_size, g_size)],
-                    send_sem.at[4],
-                    recv_sem.at[4],
+                    side_edge_out.at[:, pl.ds(j, 1)],
+                    side_edge_in.at[:, pl.ds(my_y, 1)],
+                    send_sem.at[6],
+                    recv_sem.at[6],
                     device_id=(row, j),
                     device_id_type=MESH,
                 ).start()
@@ -378,15 +481,33 @@
             return carry
 
         lax.fori_loop(0, axial, send, 0)
-        own_back.start()
+        own_side_back.start()
+
+    @pl.when(solving)
+    def _():
+        lax.fori_loop(4, axial, send_back, 0)
+
+    @pl.when(siding)
+    def _():
+        own_side_back.wait()
+        drain(side_edge_in, recv_sem.at[6], RING_Y - 1)
+
+    @pl.when(jnp.logical_not(siding))
+    def _():
+        drain(side_edge_in, recv_sem.at[6], RING_Y)
+
+    @pl.when(solving)
+    def _():
         own_back.wait()
         drain(edge_in, recv_sem.at[4], axial - g_size)
 
-    if layers != layer_count:
-
-        @pl.when(jnp.logical_not(solving))
-        def _():
-            drain(edge_in, recv_sem.at[4], axial)
+    @pl.when(jnp.logical_not(solving))
+    def _():
+        drain(edge_in, recv_sem.at[4], axial)
+
+    for k in range(2):
+        for h, g in enumerate((0, 8, 23, 31)):
+            edge_in[k, pl.ds(g, 1), :] = side_edge_in[k, pl.ds(h, 1), :]
 
     below_edge = gathered(edge_in.at[0])
     own_edge = gathered(edge_in.at[1])
@@ -410,28 +531,35 @@
         drain(rhs_out, send_sem.at[3], axial - g_size)
         drain(edge_out, send_sem.at[4], (axial - 1) * g_size)
 
-    if layers != layer_count:
-
-        @pl.when(jnp.logical_not(solving))
-        def _():
-            drain(mat_out, send_sem.at[2], axial)
-            drain(rhs_out, send_sem.at[3], axial)
+    @pl.when(jnp.logical_not(solving))
+    def _():
+        drain(mat_out, send_sem.at[2], axial)
+        drain(rhs_out, send_sem.at[3], axial)
+
+    @pl.when(siding)
+    def _():
+        drain(side_rhs_out, send_sem.at[5], RING_Y - 1)
+        drain(side_edge_out, send_sem.at[6], axial - 1)
+
+    @pl.when(jnp.logical_not(siding))
+    def _():
+        drain(side_rhs_out, send_sem.at[5], RING_Y)
 
 
 def solution(mesh):
     axial, rows = mesh.shape["axial"], mesh.shape["row"]
     layer_count = axial // RING_Y
-    layers, first_layer = 2, 0
+    first_layer = 1
 
     def on_device(warmth, supply, lower, higher, ratio, group, region, sense):
         depth, width, length = warmth.shape
         flat = (depth * width, length)
-        lines = axial * (layer_count // layers)
+        lines = axial * (layer_count // LAYERS)
         levels = axial.bit_length() - 1
         field = pltpu.VMEM(flat, jnp.float32)
         halo = pltpu.VMEM((depth, length), jnp.float32)
         out = pl.pallas_call(
-            functools.partial(kernel, axial, rows, layers, first_layer, depth),
+            functools.partial(kernel, axial, rows, first_layer, depth),
             out_shape=jax.ShapeDtypeStruct(flat, jnp.float32),
             in_specs=[pl.BlockSpec(memory_space=pltpu.HBM)] * 8,
             out_specs=pl.BlockSpec(memory_space=pltpu.VMEM),
@@ -444,6 +572,7 @@
                 pltpu.SMEM(ratio.shape, jnp.float32),
                 pltpu.SMEM(region.shape, jnp.int32),
                 pltpu.SMEM(sense.shape, jnp.int32),
+                field,
                 field,
                 field,
                 field,
@@ -460,13 +589,20 @@
                 pltpu.VMEM((2, lines, LANES), jnp.float32),
                 pltpu.VMEM((2, lines, LANES), jnp.float32),
                 pltpu.VMEM((2, axial, LANES), jnp.float32),
+                pltpu.VMEM((2, RING_Y, LANES), jnp.float32),
+                pltpu.VMEM((2, axial, LANES), jnp.float32),
+                pltpu.VMEM((2, axial, LANES), jnp.float32),
+                pltpu.VMEM((2, RING_Y, LANES), jnp.float32),
                 pltpu.VMEM((levels, lines, LANES), jnp.float32),
                 pltpu.VMEM((levels, lines, LANES), jnp.float32),
+                pltpu.VMEM((levels, axial, LANES), jnp.float32),
+                pltpu.VMEM((levels, axial, LANES), jnp.float32),
+                pltpu.VMEM((lines, LANES), jnp.float32),
                 pltpu.SemaphoreType.DMA((5,)),
                 pltpu.SemaphoreType.DMA((3,)),
-                pltpu.SemaphoreType.DMA((3,)),
                 pltpu.SemaphoreType.DMA((5,)),
-                pltpu.SemaphoreType.DMA((5,)),
+                pltpu.SemaphoreType.DMA((7,)),
+                pltpu.SemaphoreType.DMA((7,)),
             ],
             compiler_params=pltpu.CompilerParams(
                 collective_id=0, has_side_effects=True, vmem_limit_bytes=32 * 1024 * 1024

time: 22.7 us -> 21.3 us (0.938)
  Pallas kernels: 21.8 us -> 20.4 us
    pallas_call x1, Pallas kernels: 21.8 us -> 20.4 us  [on_device(): pl.pallas_call(functools.partial(kernel, axial, rows, first_layer, depth)...]
where the time goes in v3:
time: 21.3 us; the launch traced here: 21.2 us
  Pallas kernels  20.4 us (96%)
  local copies, waits for them, and re-layouts  0.8 us (4%)
    pallas_call x1, Pallas kernels, on_device(): pl.pallas_call(functools.partial(kernel, axial, rows, first_layer, depth)...  20.4 us
    unnamed x1, local copies, waits for them, and re-layouts  0.8 us

profile of v3, /device:TPU:2, one launch (start us, length us, event | category | flops | bytes accessed | tf_op | source)
XLA Modules:
  0.0 21.2 jit_solution(1930872877877952118)
XLA Ops:
  0.0 20.4 %shard_map.82 = f32[512,256]{1,0:T(8,128)S(1)} custom-call(f32[512,256]{1,0:T(8,128)} %bitcast.6, f32[512,256]{1,0:T(8,128)} %bitcast.7, f32[512,256]{1,0:T(8,128)} %bitcast.8, f32[512,256]{1,0:T(8,128)} %bitcast.9, f32[4]{0:T(128)} %ratio_hbm.1, s32[16,256]{1,0:T(8,128)} %group_hbm.1, s32[32]{0:T(128)} %region_hbm.1, s32[32]{0:T(128)} %sense_hbm.1), custom_call_target="tpu_custom_call" | custom-call | tf_op jit(solution)/shard_map/pallas_call | solution.py:561
  20.4 0.8 %copy.10 = f32[32,16,256]{2,1,0:T(8,128)} copy(f32[32,16,256]{2,1,0:T(8,128)S(1)} %bitcast.5) | data formatting | bytes 1048576

commit v4 on v3

--- a/solution.py
+++ b/solution.py
@@ -15,7 +15,9 @@
 MESH = pl.DeviceIdType.MESH
 LANES = 128
 RING_Y = 4
-LAYERS = 2
+PLACES = (0, 8, 1, 9, 12, 4, 13, 5)
+BESIDE = (0, 8, 23, 31)
+SIDES = (0, 2, 5, 7)
 
 
 def spread(ref, value):
@@ -34,7 +36,6 @@
 def kernel(
     axial,
     rows,
-    first_layer,
     depth,
     warmth_hbm,
     supply_hbm,
@@ -87,23 +88,14 @@
 ):
     me = lax.axis_index("axial")
     row = lax.axis_index("row")
-    layer_count = axial // RING_Y
-    solvers = LAYERS * RING_Y
+    solvers = len(PLACES)
     g_size = axial // solvers
-    my_y = lax.rem(me, RING_Y)
-    my_layer = lax.rem(me // RING_Y - first_layer + layer_count, layer_count)
-    my_solver = 2 * my_y + lax.rem(my_layer + my_y // 2, 2)
-    solving = my_layer < LAYERS
-    siding = my_layer == 0
+    my_solver = sum((me == place).astype(jnp.int32) * s for s, place in enumerate(PLACES))
+    solving = sum((me == place).astype(jnp.int32) for place in PLACES) > 0
+    my_side = sum((me == PLACES[s]).astype(jnp.int32) * h for h, s in enumerate(SIDES))
+    siding = sum((me == PLACES[s]).astype(jnp.int32) for s in SIDES) > 0
     has_low = row > 0
     has_high = row < rows - 1
-
-    def device_of(s):
-        layer = lax.rem(s + s // 4, 2)
-        return lax.rem(layer + first_layer, layer_count) * RING_Y + s // 2
-
-    def side_device(h):
-        return first_layer * RING_Y + h
 
     barrier = pltpu.get_barrier_semaphore()
 
@@ -236,8 +228,7 @@
             own_sem.at[which],
         )
 
-        def send(s, carry):
-            target = device_of(s)
+        for s, target in enumerate(PLACES):
 
             @pl.when(target != me)
             def _():
@@ -249,10 +240,6 @@
                     device_id=(row, target),
                     device_id_type=MESH,
                 ).start()
-
-            return carry
-
-        lax.fori_loop(0, solvers, send, 0)
 
         @pl.when(solving)
         def _():
@@ -342,11 +329,11 @@
         rhs[slab(z), :] = value
     sides(side_rhs_out.at[1], value)
     own_side = pltpu.make_async_copy(
-        side_rhs_out.at[:, pl.ds(my_y, 1)], side_rhs_in.at[:, pl.ds(me, 1)], own_sem.at[3]
-    )
-
-    def send_side(h, carry):
-        target = side_device(h)
+        side_rhs_out.at[:, pl.ds(my_side, 1)], side_rhs_in.at[:, pl.ds(me, 1)], own_sem.at[3]
+    )
+
+    for h, s in enumerate(SIDES):
+        target = PLACES[s]
 
         @pl.when(target != me)
         def _():
@@ -358,10 +345,6 @@
                 device_id=(row, target),
                 device_id_type=MESH,
             ).start()
-
-        return carry
-
-    lax.fori_loop(0, RING_Y, send_side, 0)
 
     @pl.when(siding)
     def _():
@@ -432,11 +415,11 @@
         edge_out[1] = r
         edge_out[0] = jnp.where(is_first, 0.0, down(r, 1))
 
-        lax.fori_loop(0, 4, send_back, 0)
+        lax.fori_loop(0, RING_Y, send_back, 0)
         own_back.start()
 
     own_side_back = pltpu.make_async_copy(
-        side_edge_out.at[:, pl.ds(me, 1)], side_edge_in.at[:, pl.ds(my_y, 1)], own_sem.at[4]
+        side_edge_out.at[:, pl.ds(me, 1)], side_edge_in.at[:, pl.ds(my_side, 1)], own_sem.at[4]
     )
 
     @pl.when(siding)
@@ -449,7 +432,7 @@
         def up(x, blocks):
             return pltpu.roll(x, axial - blocks, 0)
 
-        local = 3 * (my_y // 2)
+        local = (g_size - 1) * (my_side // 2)
         levels = alpha.shape[0]
         for level in range(levels):
             side_alpha[level] = alpha[level, pl.ds(local, axial, stride=g_size), :]
@@ -471,7 +454,7 @@
             def _():
                 pltpu.make_async_remote_copy(
                     side_edge_out.at[:, pl.ds(j, 1)],
-                    side_edge_in.at[:, pl.ds(my_y, 1)],
+                    side_edge_in.at[:, pl.ds(my_side, 1)],
                     send_sem.at[6],
                     recv_sem.at[6],
                     device_id=(row, j),
@@ -485,16 +468,16 @@
 
     @pl.when(solving)
     def _():
-        lax.fori_loop(4, axial, send_back, 0)
+        lax.fori_loop(RING_Y, axial, send_back, 0)
 
     @pl.when(siding)
     def _():
         own_side_back.wait()
-        drain(side_edge_in, recv_sem.at[6], RING_Y - 1)
+        drain(side_edge_in, recv_sem.at[6], len(SIDES) - 1)
 
     @pl.when(jnp.logical_not(siding))
     def _():
-        drain(side_edge_in, recv_sem.at[6], RING_Y)
+        drain(side_edge_in, recv_sem.at[6], len(SIDES))
 
     @pl.when(solving)
     def _():
@@ -506,7 +489,7 @@
         drain(edge_in, recv_sem.at[4], axial)
 
     for k in range(2):
-        for h, g in enumerate((0, 8, 23, 31)):
+        for h, g in enumerate(BESIDE):
             edge_in[k, pl.ds(g, 1), :] = side_edge_in[k, pl.ds(h, 1), :]
 
     below_edge = gathered(edge_in.at[0])
@@ -538,28 +521,26 @@
 
     @pl.when(siding)
     def _():
-        drain(side_rhs_out, send_sem.at[5], RING_Y - 1)
+        drain(side_rhs_out, send_sem.at[5], len(SIDES) - 1)
         drain(side_edge_out, send_sem.at[6], axial - 1)
 
     @pl.when(jnp.logical_not(siding))
     def _():
-        drain(side_rhs_out, send_sem.at[5], RING_Y)
+        drain(side_rhs_out, send_sem.at[5], len(SIDES))
 
 
 def solution(mesh):
     axial, rows = mesh.shape["axial"], mesh.shape["row"]
-    layer_count = axial // RING_Y
-    first_layer = 1
 
     def on_device(warmth, supply, lower, higher, ratio, group, region, sense):
         depth, width, length = warmth.shape
         flat = (depth * width, length)
-        lines = axial * (layer_count // LAYERS)
+        lines = axial * (axial // len(PLACES))
         levels = axial.bit_length() - 1
         field = pltpu.VMEM(flat, jnp.float32)
         halo = pltpu.VMEM((depth, length), jnp.float32)
         out = pl.pallas_call(
-            functools.partial(kernel, axial, rows, first_layer, depth),
+            functools.partial(kernel, axial, rows, depth),
             out_shape=jax.ShapeDtypeStruct(flat, jnp.float32),
             in_specs=[pl.BlockSpec(memory_space=pltpu.HBM)] * 8,
             out_specs=pl.BlockSpec(memory_space=pltpu.VMEM),
@@ -589,10 +570,10 @@
                 pltpu.VMEM((2, lines, LANES), jnp.float32),
                 pltpu.VMEM((2, lines, LANES), jnp.float32),
                 pltpu.VMEM((2, axial, LANES), jnp.float32),
-                pltpu.VMEM((2, RING_Y, LANES), jnp.float32),
+                pltpu.VMEM((2, len(SIDES), LANES), jnp.float32),
                 pltpu.VMEM((2, axial, LANES), jnp.float32),
                 pltpu.VMEM((2, axial, LANES), jnp.float32),
-                pltpu.VMEM((2, RING_Y, LANES), jnp.float32),
+                pltpu.VMEM((2, len(SIDES), LANES), jnp.float32),
                 pltpu.VMEM((levels, lines, LANES), jnp.float32),
                 pltpu.VMEM((levels, lines, LANES), jnp.float32),
                 pltpu.VMEM((levels, axial, LANES), jnp.float32),

time: 21.3 us -> 20.9 us (0.981)
  Pallas kernels: 20.4 us -> 20 us
    pallas_call x1, Pallas kernels: 20.4 us -> 20 us  [on_device(): pl.pallas_call(functools.partial(kernel, axial, rows, depth), out_shape=j...]
where the time goes in v4:
time: 20.9 us; the launch traced here: 20.8 us
  Pallas kernels  20 us (96%)
  local copies, waits for them, and re-layouts  0.8 us (4%)
    pallas_call x1, Pallas kernels, on_device(): pl.pallas_call(functools.partial(kernel, axial, rows, depth), out_shape=j...  20 us
    unnamed x1, local copies, waits for them, and re-layouts  0.8 us

profile of v4, /device:TPU:2, one launch (start us, length us, event | category | flops | bytes accessed | tf_op | source)
XLA Modules:
  0.0 20.8 jit_solution(6826917705095583920)
XLA Ops:
  0.0 20.0 %shard_map.82 = f32[512,256]{1,0:T(8,128)S(1)} custom-call(f32[512,256]{1,0:T(8,128)} %bitcast.6, f32[512,256]{1,0:T(8,128)} %bitcast.7, f32[512,256]{1,0:T(8,128)} %bitcast.8, f32[512,256]{1,0:T(8,128)} %bitcast.9, f32[4]{0:T(128)} %ratio_hbm.1, s32[16,256]{1,0:T(8,128)} %group_hbm.1, s32[32]{0:T(128)} %region_hbm.1, s32[32]{0:T(128)} %sense_hbm.1), custom_call_target="tpu_custom_call" | custom-call | tf_op jit(solution)/shard_map/pallas_call | solution.py:542
  20.0 0.8 %copy.10 = f32[32,16,256]{2,1,0:T(8,128)} copy(f32[32,16,256]{2,1,0:T(8,128)S(1)} %bitcast.5) | data formatting | bytes 1048576

commit v5 on v4

--- a/solution.py
+++ b/solution.py
@@ -93,6 +93,8 @@
     my_solver = sum((me == place).astype(jnp.int32) * s for s, place in enumerate(PLACES))
     solving = sum((me == place).astype(jnp.int32) for place in PLACES) > 0
     my_side = sum((me == PLACES[s]).astype(jnp.int32) * h for h, s in enumerate(SIDES))
+    kept_size = g_size - 1
+    skipped = 1 - my_side // 2
     siding = sum((me == PLACES[s]).astype(jnp.int32) for s in SIDES) > 0
     has_low = row > 0
     has_high = row < rows - 1
@@ -113,6 +115,10 @@
             pl.semaphore_signal(barrier, inc=1, device_id=(row, j), device_id_type=MESH)
 
         return carry
+
+    @pl.when(siding)
+    def _():
+        rhs_in[...] = jnp.zeros_like(rhs_in)
 
     @pl.when(solving)
     def _():
@@ -229,12 +235,15 @@
         )
 
         for s, target in enumerate(PLACES):
+            first, size = 0, g_size
+            if which == 1 and s in SIDES:
+                first, size = 1 - SIDES.index(s) // 2, kept_size
 
             @pl.when(target != me)
             def _():
                 pltpu.make_async_remote_copy(
-                    out.at[:, pl.ds(s * g_size, g_size)],
-                    into.at[:, pl.ds(me * g_size, g_size)],
+                    out.at[:, pl.ds(s * g_size + first, size)],
+                    into.at[:, pl.ds(me * g_size + first, size)],
                     send_sem.at[2 + which],
                     recv_sem.at[2 + which],
                     device_id=(row, target),
@@ -250,6 +259,24 @@
     def drain(ref, sem, count):
         part = ref.at[:, pl.ds(0, count)]
         pltpu.make_async_copy(part, part, sem).wait()
+
+    plain = jnp.logical_and(solving, jnp.logical_not(siding))
+    total = axial - len(SIDES)
+
+    def by_role(ref, sem, side_count, plain_count, other_count=None):
+        @pl.when(siding)
+        def _():
+            drain(ref, sem, side_count)
+
+        @pl.when(plain)
+        def _():
+            drain(ref, sem, plain_count)
+
+        if other_count is not None:
+
+            @pl.when(jnp.logical_not(solving))
+            def _():
+                drain(ref, sem, other_count)
 
     own_matrix = scatter(mat_out, mat_in, 0)
 
@@ -351,12 +378,12 @@
         own_side.start()
 
     lines = axial * g_size
-    def send_back(j, carry):
+    def send_back(first, size, j, carry):
         @pl.when(j != me)
         def _():
             pltpu.make_async_remote_copy(
-                edge_out.at[:, pl.ds(j * g_size, g_size)],
-                edge_in.at[:, pl.ds(my_solver * g_size, g_size)],
+                edge_out.at[:, pl.ds(j * g_size + first, size)],
+                edge_in.at[:, pl.ds(my_solver * g_size + first, size)],
                 send_sem.at[4],
                 recv_sem.at[4],
                 device_id=(row, j),
@@ -364,6 +391,15 @@
             ).start()
 
         return carry
+
+    def send_back_to(start, stop):
+        @pl.when(siding)
+        def _():
+            lax.fori_loop(start, stop, functools.partial(send_back, skipped, kept_size), 0)
+
+        @pl.when(plain)
+        def _():
+            lax.fori_loop(start, stop, functools.partial(send_back, 0, g_size), 0)
 
     own_back = pltpu.make_async_copy(
         edge_out.at[:, pl.ds(me * g_size, g_size)],
@@ -404,7 +440,7 @@
         final = 1.0 / excess
         finals[...] = final
 
-        drain(rhs_in, recv_sem.at[3], (axial - 1) * g_size)
+        by_role(rhs_in, recv_sem.at[3], (axial - 1) * kept_size, (axial - 1) * g_size)
         own_rhs.wait()
         r = rhs_in[0] + jnp.where(is_last, 0.0, up(rhs_in[1], 1))
         level, stride = 0, 1
@@ -415,7 +451,7 @@
         edge_out[1] = r
         edge_out[0] = jnp.where(is_first, 0.0, down(r, 1))
 
-        lax.fori_loop(0, RING_Y, send_back, 0)
+        send_back_to(0, RING_Y)
         own_back.start()
 
     own_side_back = pltpu.make_async_copy(
@@ -466,9 +502,7 @@
         lax.fori_loop(0, axial, send, 0)
         own_side_back.start()
 
-    @pl.when(solving)
-    def _():
-        lax.fori_loop(RING_Y, axial, send_back, 0)
+    send_back_to(RING_Y, axial)
 
     @pl.when(siding)
     def _():
@@ -479,14 +513,11 @@
     def _():
         drain(side_edge_in, recv_sem.at[6], len(SIDES))
 
+    by_role(edge_in, recv_sem.at[4], total - kept_size, total - g_size, total)
+
     @pl.when(solving)
     def _():
         own_back.wait()
-        drain(edge_in, recv_sem.at[4], axial - g_size)
-
-    @pl.when(jnp.logical_not(solving))
-    def _():
-        drain(edge_in, recv_sem.at[4], axial)
 
     for k in range(2):
         for h, g in enumerate(BESIDE):
@@ -508,16 +539,9 @@
     def _():
         to_high(device_id=(row, me)).wait_send()
 
-    @pl.when(solving)
-    def _():
-        drain(mat_out, send_sem.at[2], axial - g_size)
-        drain(rhs_out, send_sem.at[3], axial - g_size)
-        drain(edge_out, send_sem.at[4], (axial - 1) * g_size)
-
-    @pl.when(jnp.logical_not(solving))
-    def _():
-        drain(mat_out, send_sem.at[2], axial)
-        drain(rhs_out, send_sem.at[3], axial)
+    by_role(mat_out, send_sem.at[2], axial - g_size, axial - g_size, axial)
+    by_role(rhs_out, send_sem.at[3], total - kept_size, total - g_size, total)
+    by_role(edge_out, send_sem.at[4], (axial - 1) * kept_size, (axial - 1) * g_size)
 
     @pl.when(siding)
     def _():

time: 20.9 us -> 20.5 us (0.981)
  Pallas kernels: 20 us -> 19.6 us
    pallas_call x1, Pallas kernels: 20 us -> 19.6 us  [on_device(): pl.pallas_call(functools.partial(kernel, axial, rows, depth), out_shape=j...]
where the time goes in v5:
time: 20.5 us
  Pallas kernels  19.6 us (96%)
  local copies, waits for them, and re-layouts  0.8 us (4%)
    pallas_call x1, Pallas kernels, on_device(): pl.pallas_call(functools.partial(kernel, axial, rows, depth), out_shape=j...  19.6 us
    unnamed x1, local copies, waits for them, and re-layouts  0.8 us

profile of v5, /device:TPU:2, one launch (start us, length us, event | category | flops | bytes accessed | tf_op | source)
XLA Modules:
  0.0 20.5 jit_solution(2046269876248605937)
XLA Ops:
  0.0 19.6 %shard_map.82 = f32[512,256]{1,0:T(8,128)S(1)} custom-call(f32[512,256]{1,0:T(8,128)} %bitcast.6, f32[512,256]{1,0:T(8,128)} %bitcast.7, f32[512,256]{1,0:T(8,128)} %bitcast.8, f32[512,256]{1,0:T(8,128)} %bitcast.9, f32[4]{0:T(128)} %ratio_hbm.1, s32[16,256]{1,0:T(8,128)} %group_hbm.1, s32[32]{0:T(128)} %region_hbm.1, s32[32]{0:T(128)} %sense_hbm.1), custom_call_target="tpu_custom_call" | custom-call | tf_op jit(solution)/shard_map/pallas_call | solution.py:566
  19.7 0.8 %copy.10 = f32[32,16,256]{2,1,0:T(8,128)} copy(f32[32,16,256]{2,1,0:T(8,128)S(1)} %bitcast.5) | data formatting | bytes 1048576

commit v6 on v5

--- a/solution.py
+++ b/solution.py
@@ -15,7 +15,7 @@
 MESH = pl.DeviceIdType.MESH
 LANES = 128
 RING_Y = 4
-PLACES = (0, 8, 1, 9, 12, 4, 13, 5)
+PLACES = (4, 8, 5, 9, 12, 0, 13, 1)
 BESIDE = (0, 8, 23, 31)
 SIDES = (0, 2, 5, 7)
 

time: 20.5 us -> 20.4 us (level)
  no operation moved by 1% of the time
where the time goes in v6:
time: 20.4 us; the launch traced here: 20.3 us
  Pallas kernels  19.5 us (96%)
  local copies, waits for them, and re-layouts  0.8 us (4%)
    pallas_call x1, Pallas kernels, on_device(): pl.pallas_call(functools.partial(kernel, axial, rows, depth), out_shape=j...  19.5 us
    unnamed x1, local copies, waits for them, and re-layouts  0.8 us

profile of v6, /device:TPU:2, one launch (start us, length us, event | category | flops | bytes accessed | tf_op | source)
XLA Modules:
  0.0 20.3 jit_solution(13167400413931168168)
XLA Ops:
  0.0 19.5 %shard_map.82 = f32[512,256]{1,0:T(8,128)S(1)} custom-call(f32[512,256]{1,0:T(8,128)} %bitcast.6, f32[512,256]{1,0:T(8,128)} %bitcast.7, f32[512,256]{1,0:T(8,128)} %bitcast.8, f32[512,256]{1,0:T(8,128)} %bitcast.9, f32[4]{0:T(128)} %ratio_hbm.1, s32[16,256]{1,0:T(8,128)} %group_hbm.1, s32[32]{0:T(128)} %region_hbm.1, s32[32]{0:T(128)} %sense_hbm.1), custom_call_target="tpu_custom_call" | custom-call | tf_op jit(solution)/shard_map/pallas_call | solution.py:566
  19.5 0.8 %copy.10 = f32[32,16,256]{2,1,0:T(8,128)} copy(f32[32,16,256]{2,1,0:T(8,128)S(1)} %bitcast.5) | data formatting | bytes 1048576
